TPU v7x, 32 devices: a whole 2x2x4 slice. The times are simulated.
32 devices in a mesh: pipe: 8 (over z, core), dp: 4 (over y, x).
Axes of the slice: x: 2, y: 2, z: 4, core: 2. Of those that a mesh axis runs over, the one named last changes fastest.
Arguments:
- grads: bfloat16 [8, 2, 256, 8192], P('pipe', None, 'dp'), may hold values from -6 to 6
- weights: bfloat16 [8, 8192, 8192], P('pipe', 'dp'), may hold values from -0.0625 to 0.0625
- saved: bfloat16 [8, 3, 256, 8192], P('pipe', None, 'dp'), may hold values from -6 to 6
- plan: int32 [8, 2], P('pipe'), may hold values from 0 to 2, as said below
- block_of_section: int32 [8], P('pipe'), may hold values from 0 to 7, as said below
Outputs:
- upstream: bfloat16 [8, 2, 256, 8192], P('pipe', None, 'dp')
- inverse: bfloat16 [8, 512, 512], P('pipe')
Inputs may be any that keep to these rules, and one draw needn't show every extreme that they name: `plan`: each row names 2 different slots. `block_of_section`: sections name distinct block numbers where 16 >= 8; otherwise every block number is named by 0 sections.
All inputs are finite; a program needn't handle non-finite values.
Results may differ from a plain program's by a relative error of at most 0.001.
Values may be sent and summed in bfloat16 or wider, within the bound.
A program may use at most 128 MiB of HBM per device.

v0:
```python
import jax
import jax.numpy as jnp
from jax import lax
from jax.experimental import pallas as pl
from jax.experimental.pallas import tpu as pltpu
from jax.sharding import PartitionSpec as P

SUB = 8
LANES = 128


def three_parts(value):
    high = value.astype(jnp.bfloat16).astype(jnp.float32)
    rest = value - high
    mid = rest.astype(jnp.bfloat16).astype(jnp.float32)
    return high, mid, rest - mid


def exact_dot(a, b, contract):
    return lax.dot_general(
        a, b, (contract, ((), ())), precision=lax.Precision.HIGHEST, preferred_element_type=jnp.float32
    )


def invert_tile(tile):
    size = tile.shape[0]
    rows = [tile[at : at + SUB, :] for at in range(0, size, SUB)]
    lane = lax.broadcasted_iota(jnp.int32, (SUB, size), 1)
    sub = lax.broadcasted_iota(jnp.int32, (SUB, size), 0)
    for panel in range(size // SUB):
        first = panel * SUB
        old = rows[panel]
        inside = (lane >= first) & (lane < first + SUB)
        left = jnp.where(inside, 0.0, jnp.where(lane < first, -old, old))
        new = old
        for step in range(SUB):
            at = first + step
            column = jnp.broadcast_to(new[:, at : at + 1], new.shape)
            pivot = jnp.broadcast_to(column[step : step + 1, :], new.shape)
            cleared = jnp.where(lane == at, jnp.where(sub == step, 1.0, 0.0), new)
            row = jnp.broadcast_to(cleared[step : step + 1, :], new.shape) * (1.0 / pivot)
            new = jnp.where(sub == step, row, cleared - column * row)
        lh, lm, ll = three_parts(left)
        nh, nm, nl = three_parts(new)
        stacked_left = jnp.concatenate([lh, lh, lm, lh, lm, ll], axis=0).astype(jnp.bfloat16)
        stacked_new = jnp.concatenate([nh, nm, nh, nl, nm, nh], axis=0).astype(jnp.bfloat16)
        update = lax.dot_general(
            stacked_left, stacked_new, (((0,), (0,)), ((), ())), preferred_element_type=jnp.float32
        )
        rows = [
            new if at == panel else jnp.where(inside, 0.0, row) - update[at * SUB : (at + 1) * SUB, :]
            for at, row in enumerate(rows)
        ]
    return jnp.concatenate(rows, axis=0)


def invert_in_place(work):
    size = work.shape[0]

    def one_block(index, carry):
        at = pl.ds(pl.multiple_of(index * LANES, LANES), LANES)
        inverse = invert_tile(work[at, at])
        work[at, at] = jnp.zeros((LANES, LANES), jnp.float32)
        row = exact_dot(inverse, work[at, :], ((1,), (0,)))
        column = work[:, at]
        work[:, at] = jnp.zeros((size, LANES), jnp.float32)
        work[at, :] = row
        work[at, at] = inverse
        full = work[at, :]
        work[at, :] = jnp.zeros((LANES, size), jnp.float32)
        work[...] = work[...] - exact_dot(column, full, ((1,), (0,)))
        work[at, :] = full
        return carry

    lax.fori_loop(0, size // LANES, one_block, 0)


def inverse_kernel(rows_ref, out_ref, work):
    size = work.shape[0]
    gram = lax.dot_general(
        rows_ref[...], rows_ref[...], (((0,), (0,)), ((), ())), preferred_element_type=jnp.float32
    )
    down = lax.broadcasted_iota(jnp.int32, (size, size), 0)
    across = lax.broadcasted_iota(jnp.int32, (size, size), 1)
    work[...] = gram / rows_ref.shape[0] + jnp.where(down == across, 1.0, 0.0)
    invert_in_place(work)
    out_ref[...] = work[...].astype(out_ref.dtype)


def inverse_of(all_rows):
    size = all_rows.shape[1]
    return pl.pallas_call(
        inverse_kernel,
        out_shape=jax.ShapeDtypeStruct((size, size), jnp.bfloat16),
        scratch_shapes=[pltpu.VMEM((size, size), jnp.float32)],
        compiler_params=pltpu.CompilerParams(vmem_limit_bytes=24 * 1024 * 1024),
        cost_estimate=pl.CostEstimate(flops=10**9, bytes_accessed=150 * 10**6, transcendentals=0),
    )(all_rows)

BLK = 512


def passed_along(value, axis, steps):
    count = lax.axis_size(axis)
    first, last = (max(0, -steps), min(count, count - steps))
    return lax.ppermute(value, axis, [(source, source + steps) for source in range(first, last)])


def on_device(grads, weights, saved, plan, block_of_section):
    weight_rows = weights[0]
    columns = jnp.einsum(
        "amtd,id->amti",
        lax.all_gather(grads, "dp", axis=2, tiled=True),
        weight_rows,
        preferred_element_type=jnp.float32,
    ).astype(jnp.bfloat16)
    mine = lax.all_to_all(columns, "dp", split_axis=2, concat_axis=3, tiled=True)
    upstream = passed_along(mine, "pipe", -1)
    block = block_of_section[0]
    selected = lax.dynamic_slice_in_dim(saved[0], block * BLK, BLK, 2)
    picked = jnp.take(selected, plan[0], axis=0).reshape(-1, BLK)
    all_rows = lax.all_gather(picked, "dp", axis=0, tiled=True)
    inverse = inverse_of(all_rows)
    return (upstream, inverse[None])


def solution(mesh):
    in_specs = (
        P("pipe", None, "dp", None),
        P("pipe", "dp", None),
        P("pipe", None, "dp", None),
        P("pipe", None),
        P("pipe"),
    )
    out_specs = (P("pipe", None, "dp", None), P("pipe", None, None))
    return jax.shard_map(
        on_device, mesh=mesh, in_specs=in_specs, out_specs=out_specs, check_vma=False
    )
```

profile of v0, /device:TPU:8, one launch (start us, length us, event | category | flops | bytes accessed | tf_op | source)
XLA Modules:
  0.0 256.3 jit_solution(5426032958056539258)
XLA Ops:
  7.2 0.0 copy-start
  7.2 0.0 all-gather.2.cloned.1.call-start
  7.2 0.7 all-gather.2.cloned.1.call-update
  7.9 90.8 %all-gather.2.cloned.1.call-done = bf16[1,2,256,8192]{3,2,1,0:T(8,128)(2,1)} async-done(((bf16[1,2,64,8192]{3,2,1,0:T(8,128)(2,1)}), bf16[1,2,256,8192]{3,2,1,0:T(8,128)(2,1)}) %all-gather.2.cloned.1.call-update) | async-done | bytes 8388624 | tf_op jit(solution)/shard_map/all_gather | solution.py:113
  98.7 23.9 %fusion.8 = bf16[1,2,256,2048]{3,2,1,0:T(8,128)(2,1)S(1)} fusion(bf16[1,2048,8192]{2,1,0:T(8,128)(2,1)} %param.6, bf16[1,2,256,8192]{3,2,1,0:T(8,128)(2,1)} %all-gather.2.cloned.1.call-done), kind=kOutput, calls=%fused_computation.5 | convolution fusion | flops 17180917760 | bytes 44040192 | tf_op jit(solution)/shard_map/amtd,id->amti/dot_general | solution.py:111
  122.6 2.2 copy.8
  124.7 28.1 %all_to_all.18 = bf16[1,2,256,2048]{3,1,0,2:T(2,128)(2,1)S(1)} all-to-all(bf16[1,2,256,2048]{3,1,0,2:T(2,128)(2,1)S(1)} %copy.8), channel_id=1, replica_groups=mesh['pipe'=8,'dp'=4] {'dp'}, dimensions={2} | all-to-all | bytes 4194304 | tf_op jit(solution)/shard_map/all_to_all | solution.py:117
  152.9 3.0 %copy.9 = bf16[1,2,64,4,2048]{4,3,2,1,0:T(4,128)(2,1)} copy(bf16[1,2,64,4,2048]{4,1,2,3,0:T(2,128)(2,1)S(1)} %bitcast.32) | data formatting | bytes 4194304 | tf_op jit(solution)/shard_map/all_to_all | solution.py:117
  155.8 0.0 copy-start.1
  155.8 4.4 %all_to_all.16 = bf16[1,2,64,8192]{3,2,1,0:T(8,128)(2,1)} reshape(bf16[1,2,64,4,2048]{4,3,2,1,0:T(4,128)(2,1)} %copy.9) | data formatting | bytes 4194304 | tf_op jit(solution)/shard_map/all_to_all | solution.py:117
  160.3 1.9 collective-permute-start
  162.8 0.0 copy-done.1
  162.9 0.1 broadcast_in_dim.17
  162.9 0.1 broadcast_in_dim.18
  163.0 0.0 copy-done
  163.1 0.6 gather_fusion
  163.6 0.1 bitcast_select_fusion
  163.7 10.3 %all_gather.7.rows_ref = bf16[512,512]{1,0:T(8,128)(2,1)S(1)} all-gather(bf16[128,512]{1,0:T(8,128)(2,1)S(1)} %bitcast_select_fusion), channel_id=1, replica_groups=mesh['pipe'=8,'dp'=4] {'dp'}, dimensions={0}, use_global_device_ids=true | all-gather | bytes 655360 | tf_op jit(solution)/shard_map/all_gather | solution.py:122
  174.0 72.3 %shard_map.68 = bf16[512,512]{1,0:T(8,128)(2,1)} custom-call(bf16[512,512]{1,0:T(8,128)(2,1)S(1)} %all_gather.7.rows_ref), custom_call_target="tpu_custom_call" | custom-call | flops 1000000000 | bytes 150000000 | tf_op jit(solution)/shard_map/pallas_call | solution.py:92
  246.3 0.0 collective-permute-done
  246.3 3.1 %copy.12 = bf16[1,2,64,8192]{3,2,1,0:T(8,128)(2,1)} copy(bf16[1,2,64,8192]{3,2,1,0:T(8,128)(2,1)} %collective-permute-done) | data formatting | bytes 4194304
  (4 shorter events, 0.0 us)
Async XLA Ops:
  7.2 155.9 %copy-start = (bf16[1,3,64,8192]{3,2,1,0:T(8,128)(2,1)S(1)}, bf16[1,3,64,8192]{3,2,1,0:T(8,128)(2,1)}, u32[]{:S(2)}) copy-start(bf16[1,3,64,8192]{3,2,1,0:T(8,128)(2,1)} %param.7) | copy-start | bytes 9437188
  7.2 91.5 %all-gather.2.cloned.1.call-start = ((), (), s32[]{:S(2)}) async-start(), calls=%async_computation.1 | async-start | bytes 10485760 | tf_op jit(solution)/shard_map/all_gather | solution.py:113
  155.8 7.0 %copy-start.1 = (s32[1,2]{1,0:T(1,128)S(1)}, s32[1,2]{1,0:T(1,128)}, u32[]{:S(2)}) copy-start(s32[1,2]{1,0:T(1,128)} %param.8) | copy-start | bytes 28
  160.3 86.1 %collective-permute-start = (bf16[1,2,64,8192]{3,2,1,0:T(8,128)(2,1)}, bf16[1,2,64,8192]{3,2,1,0:T(8,128)(2,1)}, u32[]{:S(2)}, u32[]{:S(2)}) collective-permute-start(bf16[1,2,64,8192]{3,2,1,0:T(8,128)(2,1)} %all_to_all.16), channel_id=1, source_target_pairs={{4,0},{8,4},{12,8},{16,12},{20,16},{24,20},{28,24},{5,1},{9,5},{13... | collective-permute-start | bytes 6291464 | tf_op jit(solution)/shard_map/ppermute | solution.py:106
Sparse Core Ops, SparseCore 0:
  9.9 88.7 all-gather.1
where the time goes:
time: 258 us; the launch traced here: 256 us
  waiting for transfers between devices  91.4 us (35%)
  Pallas kernels  72.3 us (28%)
  blocking collectives  38.4 us (15%)
  matrix products  23.9 us (9%)
  between operations  14.8 us (6%)
  local copies, waits for them, and re-layouts  13.4 us (5%)
    all_gather x1, waiting for transfers between devices, on_device(): lax.all_gather(grads, 'dp', axis=2, tiled=True)  90.8 us
    pallas_call x1, Pallas kernels, inverse_of(): pl.pallas_call(inverse_kernel, out_shape=jax.ShapeDtypeStruct((size, size...  72.3 us
    all_to_all x1, blocking collectives, on_device(): lax.all_to_all(columns, 'dp', split_axis=2, concat_axis=3, tiled=True)  28.1 us
    dot_general x1, matrix products, on_device(): jnp.einsum('amtd,id->amti', lax.all_gather(grads, 'dp', axis=2, tiled=Tru...  23.9 us
    all_gather x1, blocking collectives, on_device(): all_rows = lax.all_gather(picked, 'dp', axis=0, tiled=True)  10.3 us
    all_to_all x2, local copies, waits for them, and re-layouts, on_device(): lax.all_to_all(columns, 'dp', split_axis=2, concat_axis=3, tiled=True)  7.4 us
  transfers between devices with their start and end apart: 2, of which 1 were waited for; matrix products, arithmetic and copies ran while one was open for 0% of the time, Pallas kernels for 28%

commit v1 on v0

v1 whole, which is shorter than its diff:
```python
import functools

import jax
import jax.numpy as jnp
from jax import lax
from jax.experimental import pallas as pl
from jax.experimental.pallas import tpu as pltpu
from jax.sharding import PartitionSpec as P

BLK = 512
SUB = 8
TILE = 256
PIECES = 2
LANES = 128


def three_parts(value):
    high = value.astype(jnp.bfloat16).astype(jnp.float32)
    rest = value - high
    mid = rest.astype(jnp.bfloat16).astype(jnp.float32)
    return high, mid, rest - mid


def exact_dot(a, b, contract):
    return lax.dot_general(
        a, b, (contract, ((), ())), precision=lax.Precision.HIGHEST, preferred_element_type=jnp.float32
    )


def invert_tile(tile):
    size = tile.shape[0]
    rows = [tile[at : at + SUB, :] for at in range(0, size, SUB)]
    lane = lax.broadcasted_iota(jnp.int32, (SUB, size), 1)
    sub = lax.broadcasted_iota(jnp.int32, (SUB, size), 0)
    spread = lambda value, at: jnp.broadcast_to(value[at : at + 1, :], value.shape)
    across = lambda value, at: jnp.broadcast_to(value[:, at : at + 1], value.shape)
    old = rows[0]
    for panel in range(size // SUB):
        first = panel * SUB
        inside = (lane >= first) & (lane < first + SUB)
        left = jnp.where(inside, 0.0, jnp.where(lane < first, -old, old))
        columns = [across(old, first + step) for step in range(SUB)]
        new = jnp.where(inside, jnp.where(lane - first == sub, 1.0, 0.0), old)
        for step in range(SUB):
            column = columns[step]
            scale = 1.0 / spread(column, step)
            here = sub == step

            def eliminate(value):
                row = spread(value, step) * scale
                return jnp.where(here, row, value - column * row)

            new = eliminate(new)
            for later in range(step + 1, SUB):
                columns[later] = eliminate(columns[later])
        if panel + 1 < size // SUB:
            following = rows[panel + 1]
            ahead = jnp.where(inside, 0.0, following)
            for step in range(SUB):
                ahead = ahead - across(following, first + step) * spread(new, step)
        lh, lm, ll = three_parts(left)
        nh, nm, nl = three_parts(new)
        stacked_left = jnp.concatenate([lh, lh, lm, lh, lm, ll], axis=0).astype(jnp.bfloat16)
        stacked_new = jnp.concatenate([nh, nm, nh, nl, nm, nh], axis=0).astype(jnp.bfloat16)
        update = lax.dot_general(
            stacked_left, stacked_new, (((0,), (0,)), ((), ())), preferred_element_type=jnp.float32
        )
        rows = [
            new if at == panel else jnp.where(inside, 0.0, row) - update[at * SUB : (at + 1) * SUB, :]
            for at, row in enumerate(rows)
        ]
        if panel + 1 < size // SUB:
            rows[panel + 1] = old = ahead
    return jnp.concatenate(rows, axis=0)


def invert_in_place(work):
    size = work.shape[0]

    def one_block(index, carry):
        at = pl.ds(pl.multiple_of(index * LANES, LANES), LANES)
        inverse = invert_tile(work[at, at])
        work[at, at] = jnp.zeros((LANES, LANES), jnp.float32)
        row = exact_dot(inverse, work[at, :], ((1,), (0,)))
        column = work[:, at]
        work[:, at] = jnp.zeros((size, LANES), jnp.float32)
        work[at, :] = row
        work[at, at] = inverse
        full = work[at, :]
        work[at, :] = jnp.zeros((LANES, size), jnp.float32)
        work[...] = work[...] - exact_dot(column, full, ((1,), (0,)))
        work[at, :] = full
        return carry

    lax.fori_loop(0, size // LANES, one_block, 0)


def relay_kernel(
    sections, peers, grads, weights, picked, upstream, inverse,
    shards, held, results, rows, work, zeros,
    own_sem, weight_sem, shard_send, shard_recv, row_send, row_recv, out_send, out_recv, zero_sem,
):
    section, me = lax.axis_index("pipe"), lax.axis_index("dp")
    micro, tokens, depth = shards.shape[1:]
    outs = held.shape[0]
    part = outs // PIECES
    tile = min(TILE, part)
    relayed = peers == 4

    def peer(slot):
        if relayed:
            return (me // 2 + slot // 2) % 2 * 2 + (me % 2 + slot % 2) % 2
        return (me + slot) % peers

    def beside(slot):
        return (section, peer(slot))

    barrier = pltpu.get_barrier_semaphore()
    for slot in range(1, peers):
        pl.semaphore_signal(barrier, inc=1, device_id=beside(slot), device_id_type=pl.DeviceIdType.MESH)

    for other in ((section + 1) % sections, (section + sections - 1) % sections):
        for slot in range(peers):
            pl.semaphore_signal(
                barrier, inc=1, device_id=(other, peer(slot)), device_id_type=pl.DeviceIdType.MESH
            )
    pl.semaphore_wait(barrier, 3 * peers - 1)

    def remote(source, target, send, recv, device):
        return pltpu.make_async_remote_copy(
            src_ref=source, dst_ref=target, send_sem=send, recv_sem=recv,
            device_id=device, device_id_type=pl.DeviceIdType.MESH,
        )

    def row_copy(slot):
        return remote(picked, rows.at[slot], row_send.at[slot], row_recv.at[slot], beside(slot))

    def shard_copy(slot, batch):
        return remote(
            grads.at[0, batch], shards.at[slot, batch],
            shard_send.at[slot, batch], shard_recv.at[slot, batch], beside(slot),
        )

    def relay_copy(batch):
        source, onward = (1, 2) if batch == 0 else (2, 1)
        return remote(
            shards.at[source, batch], shards.at[3, batch],
            shard_send.at[3, batch], shard_recv.at[3, batch], beside(onward),
        )

    def weight_copy(at):
        where = pl.ds(pl.multiple_of(at * tile, tile), tile)
        return pltpu.make_async_copy(weights.at[0, where, :], held.at[where, :], weight_sem.at[at])

    def result_copy(slot, piece):
        where = pl.ds(pl.multiple_of(me * outs + piece * part, part), part)
        return remote(
            results.at[slot, piece], upstream.at[0, :, :, where],
            out_send.at[slot, piece], out_recv.at[slot, piece], (section - 1, peer(slot)),
        )

    def zero_copy(at):
        return pltpu.make_async_copy(zeros, upstream.at[0, :, :, pl.ds(at * outs, outs)], zero_sem.at[at])

    for slot in range(1, peers):
        row_copy(slot).start()
    direct = range(1, 3) if relayed else range(1, peers)
    for turn in range(micro):
        for slot in direct:
            shard_copy(slot, turn if slot % 2 else micro - 1 - turn).start()
    own = pltpu.make_async_copy(grads.at[0], shards.at[0], own_sem.at[0])
    own.start()
    own_rows = pltpu.make_async_copy(picked, rows.at[0], own_sem.at[1])
    own_rows.start()
    lax.fori_loop(0, outs // tile, lambda at, carry: (weight_copy(at).start(), carry)[1], 0)

    @pl.when(section == sections - 1)
    def _():
        zeros[...] = jnp.zeros(zeros.shape, zeros.dtype)
        for at in range(peers):
            zero_copy(at).start()

    def multiply(first, count):
        for piece in range(PIECES):

            def one_tile(step, carry):
                at = piece * (part // tile) + step
                if first == 0:
                    weight_copy(at).wait()
                total = lax.dot_general(
                    shards[first : first + count].reshape(count * micro * tokens, depth),
                    held[pl.ds(pl.multiple_of(at * tile, tile), tile), :],
                    (((1,), (1,)), ((), ())),
                    preferred_element_type=jnp.float32,
                )
                results[first : first + count, piece, :, :, pl.ds(pl.multiple_of(step * tile, tile), tile)] = (
                    total.astype(results.dtype).reshape(count, micro, tokens, tile)
                )
                return carry

            lax.fori_loop(0, part // tile, one_tile, 0)

            @pl.when(section > 0)
            def _():
                for slot in range(first, first + count):
                    result_copy(slot, piece).start()

    own.wait()
    multiply(0, 1)

    own_rows.wait()
    for slot in range(1, peers):
        row_copy(slot).wait_recv()
    size = work.shape[0]
    flat = rows[...].reshape(-1, size)
    gram = lax.dot_general(flat, flat, (((0,), (0,)), ((), ())), preferred_element_type=jnp.float32)
    down = lax.broadcasted_iota(jnp.int32, (size, size), 0)
    along = lax.broadcasted_iota(jnp.int32, (size, size), 1)
    work[...] = gram / flat.shape[0] + jnp.where(down == along, 1.0, 0.0)
    invert_in_place(work)
    inverse[0] = work[...].astype(inverse.dtype)

    arrived = set()

    def arrive(slot, batch):
        if (slot, batch) not in arrived:
            arrived.add((slot, batch))
            shard_copy(slot, batch).wait_recv()

    if relayed:
        for batch in range(micro):
            arrive(1 if batch == 0 else 2, batch)
            relay_copy(batch).start()
    at = 1
    while at < peers:
        count = min(2, peers - at)
        for slot in range(at, at + count):
            for batch in range(micro):
                arrive(slot, batch)
        multiply(at, count)
        at += count

    for slot in range(1, peers):
        row_copy(slot).wait_send()
        for batch in range(micro):
            shard_copy(slot, batch).wait_send()

    @pl.when(section > 0)
    def _():
        for slot in range(peers):
            for piece in range(PIECES):
                result_copy(slot, piece).wait_send()

    @pl.when(section < sections - 1)
    def _():
        for slot in range(peers):
            for piece in range(PIECES):
                result_copy(slot, piece).wait_recv()

    @pl.when(section == sections - 1)
    def _():
        for at in range(peers):
            zero_copy(at).wait()


def relay(sections, peers, grads, weights, picked):
    micro, tokens, depth = grads.shape[1:]
    outs = weights.shape[1]
    part = outs // PIECES
    size = picked.shape[1]
    dma = pltpu.SemaphoreType.DMA
    anywhere = pl.BlockSpec(memory_space=pl.ANY)
    return pl.pallas_call(
        functools.partial(relay_kernel, sections, peers),
        out_shape=(
            jax.ShapeDtypeStruct(grads.shape, grads.dtype),
            jax.ShapeDtypeStruct((1, size, size), jnp.bfloat16),
        ),
        in_specs=[anywhere] * 3,
        out_specs=(anywhere, pl.BlockSpec(memory_space=pltpu.VMEM)),
        scratch_shapes=[
            pltpu.VMEM((peers, micro, tokens, depth), grads.dtype),
            pltpu.VMEM((outs, depth), weights.dtype),
            pltpu.VMEM((peers, PIECES, micro, tokens, part), grads.dtype),
            pltpu.VMEM((peers,) + picked.shape, picked.dtype),
            pltpu.VMEM((size, size), jnp.float32),
            pltpu.VMEM((micro, tokens, outs), grads.dtype),
            dma((2,)),
            dma((outs // min(TILE, part),)),
            dma((peers, micro)),
            dma((peers, micro)),
            dma((peers,)),
            dma((peers,)),
            dma((peers, PIECES)),
            dma((peers, PIECES)),
            dma((peers,)),
        ],
        compiler_params=pltpu.CompilerParams(
            collective_id=0, has_side_effects=True, vmem_limit_bytes=58 * 1024 * 1024
        ),
        cost_estimate=pl.CostEstimate(
            flops=2 * peers * micro * tokens * outs * depth,
            bytes_accessed=2 * outs * depth,
            transcendentals=0,
        ),
    )(grads, weights, picked)


def on_device(grads, weights, saved, plan, block_of_section):
    tokens = saved.shape[2]
    column = block_of_section[0] * BLK
    picked = jnp.concatenate(
        [
            lax.dynamic_slice(saved, (0, plan[0, batch], 0, column), (1, 1, tokens, BLK))[0, 0]
            for batch in range(plan.shape[1])
        ],
        axis=0,
    )
    return relay(lax.axis_size("pipe"), lax.axis_size("dp"), grads, weights, picked)


def solution(mesh):
    in_specs = (
        P("pipe", None, "dp", None),
        P("pipe", "dp", None),
        P("pipe", None, "dp", None),
        P("pipe", None),
        P("pipe"),
    )
    out_specs = (P("pipe", None, "dp", None), P("pipe", None, None))
    return jax.shard_map(
        on_device, mesh=mesh, in_specs=in_specs, out_specs=out_specs, check_vma=False
    )
```

time: 258 us -> 117 us (0.45)
  waiting for transfers between devices: 91.4 us -> 0 us
  blocking collectives: 38.4 us -> 0 us
  Pallas kernels: 72.3 us -> 105 us
  matrix products: 23.9 us -> 0 us
  between operations: 14.8 us -> 5.18 us
  local copies, waits for them, and re-layouts: 13.4 us -> 6.15 us
    all_gather x1 -> x0, waiting for transfers between devices: 90.8 us -> none  [on_device(): lax.all_gather(grads, 'dp', axis=2, tiled=True)]
    pallas_call x1, Pallas kernels: 72.3 us -> 105 us  [relay(): pl.pallas_call(functools.partial(relay_kernel, sections, peers), out_shap...]
    all_to_all x1 -> x0, blocking collectives: 28.1 us -> none  [on_device(): lax.all_to_all(columns, 'dp', split_axis=2, concat_axis=3, tiled=True)]
    dot_general x1 -> x0, matrix products: 23.9 us -> none  [on_device(): jnp.einsum('amtd,id->amti', lax.all_gather(grads, 'dp', axis=2, tiled=Tru...]
    all_gather x1 -> x0, blocking collectives: 10.3 us -> none  [on_device(): all_rows = lax.all_gather(picked, 'dp', axis=0, tiled=True)]
    all_to_all x2 -> x0, local copies, waits for them, and re-layouts: 7.4 us -> none  [on_device(): lax.all_to_all(columns, 'dp', split_axis=2, concat_axis=3, tiled=True)]
  transfers between devices with their start and end apart: 2 -> 0, of which waited for: 1 -> 0; matrix products, arithmetic and copies ran while one was open for 0% -> 0% of each run, Pallas kernels for 28% -> 0%
where the time goes in v1:
time: 117 us
  Pallas kernels  105 us (90%)
  local copies, waits for them, and re-layouts  6.15 us (5%)
  between operations  5.18 us (4%)
    pallas_call x1, Pallas kernels, relay(): pl.pallas_call(functools.partial(relay_kernel, sections, peers), out_shap...  105 us
    unnamed x4, local copies, waits for them, and re-layouts  3.95 us

profile of v1, /device:TPU:8, one launch (start us, length us, event | category | flops | bytes accessed | tf_op | source)
XLA Modules:
  0.0 117.1 jit_solution(15297934148095901065)
XLA Ops:
  1.3 1.3 %fusion = (s32[1,1]{1,0:T(1,128)}, s32[1,1]{1,0:T(1,128)}) fusion(s32[1,2]{1,0:T(1,128)} %param.8), kind=kLoop, calls=%fused_computation.3 | loop fusion | bytes 16 | tf_op jit(solution)/shard_map/slice | solution.py:314
  6.5 0.9 dynamic-slice_bitcast_fusion.1
  7.4 0.7 pad_maximum_fusion.picked
  8.0 105.0 %shard_map.68 = (bf16[1,2,64,8192]{3,2,1,0:T(8,128)(2,1)}, bf16[1,512,512]{2,1,0:T(8,128)(2,1)}) custom-call(bf16[1,2,64,8192]{3,2,1,0:T(8,128)(2,1)} %grads.1, bf16[1,2048,8192]{2,1,0:T(8,128)(2,1)} %weights.1, bf16[128,512]{1,0:T(8,128)(2,1)} %pad_maximum_fusion.picked), custom_call_target="tpu_custom_call" | custom-call | flops 17179869184 | bytes 33554432 | tf_op jit(solution)/shard_map/pallas_call | solution.py:273
  113.1 0.0 copy-start
  113.1 3.2 %copy.10 = bf16[1,2,64,8192]{3,2,1,0:T(8,128)(2,1)} copy(bf16[1,2,64,8192]{3,2,1,0:T(8,128)(2,1)} %get-tuple-element.8) | data formatting | bytes 4194304
  116.3 0.0 copy-done
  116.3 0.8 copy.11
Async XLA Ops:
  113.1 3.2 %copy-start = (bf16[1,512,512]{2,1,0:T(8,128)(2,1)S(1)}, bf16[1,512,512]{2,1,0:T(8,128)(2,1)}, u32[]{:S(2)}) copy-start(bf16[1,512,512]{2,1,0:T(8,128)(2,1)} %get-tuple-element.9) | copy-start | bytes 1572868

commit v2 on v1

--- a/solution.py
+++ b/solution.py
@@ -10,7 +10,7 @@
 BLK = 512
 SUB = 8
 TILE = 256
-PIECES = 2
+PIECES = 4
 LANES = 128
 
 
@@ -74,7 +74,7 @@
     return jnp.concatenate(rows, axis=0)
 
 
-def invert_in_place(work):
+def eliminate_blocks(work, first, end):
     size = work.shape[0]
 
     def one_block(index, carry):
@@ -92,13 +92,13 @@
         work[at, :] = full
         return carry
 
-    lax.fori_loop(0, size // LANES, one_block, 0)
+    lax.fori_loop(first, end, one_block, 0)
 
 
 def relay_kernel(
     sections, peers, grads, weights, picked, upstream, inverse,
     shards, held, results, rows, work, zeros,
-    own_sem, weight_sem, shard_send, shard_recv, row_send, row_recv, out_send, out_recv, zero_sem,
+    own_sem, weight_sem, shard_send, shard_recv, row_sem, row_send, row_recv, out_send, out_recv, zero_sem,
 ):
     section, me = lax.axis_index("pipe"), lax.axis_index("dp")
     micro, tokens, depth = shards.shape[1:]
@@ -115,6 +115,11 @@
     def beside(slot):
         return (section, peer(slot))
 
+    own_rows = pltpu.make_async_copy(picked, rows.at[0], row_sem)
+    own_rows.start()
+    own = pltpu.make_async_copy(grads.at[0], shards.at[0], own_sem)
+    own.start()
+
     barrier = pltpu.get_barrier_semaphore()
     for slot in range(1, peers):
         pl.semaphore_signal(barrier, inc=1, device_id=beside(slot), device_id_type=pl.DeviceIdType.MESH)
@@ -162,16 +167,13 @@
     def zero_copy(at):
         return pltpu.make_async_copy(zeros, upstream.at[0, :, :, pl.ds(at * outs, outs)], zero_sem.at[at])
 
+    def send_shards(turn):
+        for slot in range(1, 3) if relayed else range(1, peers):
+            shard_copy(slot, turn if slot % 2 else micro - 1 - turn).start()
+
     for slot in range(1, peers):
         row_copy(slot).start()
-    direct = range(1, 3) if relayed else range(1, peers)
-    for turn in range(micro):
-        for slot in direct:
-            shard_copy(slot, turn if slot % 2 else micro - 1 - turn).start()
-    own = pltpu.make_async_copy(grads.at[0], shards.at[0], own_sem.at[0])
-    own.start()
-    own_rows = pltpu.make_async_copy(picked, rows.at[0], own_sem.at[1])
-    own_rows.start()
+    send_shards(0)
     lax.fori_loop(0, outs // tile, lambda at, carry: (weight_copy(at).start(), carry)[1], 0)
 
     @pl.when(section == sections - 1)
@@ -207,6 +209,8 @@
 
     own.wait()
     multiply(0, 1)
+    for turn in range(1, micro):
+        send_shards(turn)
 
     own_rows.wait()
     for slot in range(1, peers):
@@ -217,8 +221,8 @@
     down = lax.broadcasted_iota(jnp.int32, (size, size), 0)
     along = lax.broadcasted_iota(jnp.int32, (size, size), 1)
     work[...] = gram / flat.shape[0] + jnp.where(down == along, 1.0, 0.0)
-    invert_in_place(work)
-    inverse[0] = work[...].astype(inverse.dtype)
+    blocks = size // LANES
+    eliminate_blocks(work, 0, blocks // 2)
 
     arrived = set()
 
@@ -231,6 +235,7 @@
         for batch in range(micro):
             arrive(1 if batch == 0 else 2, batch)
             relay_copy(batch).start()
+    eliminate_blocks(work, blocks // 2, blocks - 1)
     at = 1
     while at < peers:
         count = min(2, peers - at)
@@ -240,6 +245,8 @@
         multiply(at, count)
         at += count
 
+    eliminate_blocks(work, blocks - 1, blocks)
+    inverse[0] = work[...].astype(inverse.dtype)
     for slot in range(1, peers):
         row_copy(slot).wait_send()
         for batch in range(micro):
@@ -267,7 +274,7 @@
     micro, tokens, depth = grads.shape[1:]
     outs = weights.shape[1]
     part = outs // PIECES
-    size = picked.shape[1]
+    size = BLK
     dma = pltpu.SemaphoreType.DMA
     anywhere = pl.BlockSpec(memory_space=pl.ANY)
     return pl.pallas_call(
@@ -285,10 +292,11 @@
             pltpu.VMEM((peers,) + picked.shape, picked.dtype),
             pltpu.VMEM((size, size), jnp.float32),
             pltpu.VMEM((micro, tokens, outs), grads.dtype),
-            dma((2,)),
+            dma,
             dma((outs // min(TILE, part),)),
             dma((peers, micro)),
             dma((peers, micro)),
+            dma,
             dma((peers,)),
             dma((peers,)),
             dma((peers, PIECES)),
@@ -306,17 +314,63 @@
     )(grads, weights, picked)
 
 
+def copy_kernel(first, second, first_out, second_out, sems):
+    copies = [
+        pltpu.make_async_copy(first, first_out, sems.at[0]),
+        pltpu.make_async_copy(second, second_out, sems.at[1]),
+    ]
+    for copy in copies:
+        copy.start()
+    for copy in copies:
+        copy.wait()
+
+
+def handed_over(first, second):
+    anywhere = pl.BlockSpec(memory_space=pl.ANY)
+    return pl.pallas_call(
+        copy_kernel,
+        out_shape=(
+            jax.ShapeDtypeStruct(first.shape, first.dtype),
+            jax.ShapeDtypeStruct(second.shape, second.dtype),
+        ),
+        in_specs=[anywhere] * 2,
+        out_specs=(anywhere, anywhere),
+        scratch_shapes=[pltpu.SemaphoreType.DMA((2,))],
+        compiler_params=pltpu.CompilerParams(vmem_limit_bytes=58 * 1024 * 1024),
+    )(first, second)
+
+
+def pick_kernel(plan, block, saved, picked, sems):
+    micro, tokens = plan.shape[1], saved.shape[2]
+    column = pl.ds(pl.multiple_of(block[0] * BLK, BLK), BLK)
+    copies = [
+        pltpu.make_async_copy(
+            saved.at[0, plan[0, batch], :, column], picked.at[pl.ds(batch * tokens, tokens), :], sems.at[batch]
+        )
+        for batch in range(micro)
+    ]
+    for copy in copies:
+        copy.start()
+    for copy in copies:
+        copy.wait()
+
+
+def pick(saved, plan, block):
+    anywhere = pl.BlockSpec(memory_space=pl.ANY)
+    scalars = pl.BlockSpec(memory_space=pltpu.SMEM)
+    return pl.pallas_call(
+        pick_kernel,
+        out_shape=jax.ShapeDtypeStruct((plan.shape[1] * saved.shape[2], BLK), saved.dtype),
+        in_specs=[scalars, scalars, anywhere],
+        out_specs=anywhere,
+        scratch_shapes=[pltpu.SemaphoreType.DMA((plan.shape[1],))],
+        compiler_params=pltpu.CompilerParams(vmem_limit_bytes=58 * 1024 * 1024),
+    )(plan, block, saved)
+
+
 def on_device(grads, weights, saved, plan, block_of_section):
-    tokens = saved.shape[2]
-    column = block_of_section[0] * BLK
-    picked = jnp.concatenate(
-        [
-            lax.dynamic_slice(saved, (0, plan[0, batch], 0, column), (1, 1, tokens, BLK))[0, 0]
-            for batch in range(plan.shape[1])
-        ],
-        axis=0,
-    )
-    return relay(lax.axis_size("pipe"), lax.axis_size("dp"), grads, weights, picked)
+    picked = pick(saved, plan, block_of_section)
+    return handed_over(*relay(lax.axis_size("pipe"), lax.axis_size("dp"), grads, weights, picked))
 
 
 def solution(mesh):

time: 117 us -> 194 us (1.66); the launches traced: 117 us -> 190 us
  Pallas kernels: 105 us -> 189 us
  local copies, waits for them, and re-layouts: 6.15 us -> 0 us
  between operations: 5.18 us -> 1.45 us
    pallas_call x0 -> x2, Pallas kernels: none -> 86.3 us  [the longest x1 80.5 us: handed_over(): pl.pallas_call(copy_kernel, out_shape=(jax.ShapeDtypeStruct(first.shape,...]
    unnamed x4 -> x0, local copies, waits for them, and re-layouts: 3.95 us -> none
    pallas_call x1, Pallas kernels: 105 us -> 102 us  [relay(): pl.pallas_call(functools.partial(relay_kernel, sections, peers), out_shap...]
where the time goes in v2:
time: 194 us; the launch traced here: 190 us
  Pallas kernels  189 us (97%)
    pallas_call x1, Pallas kernels, relay(): pl.pallas_call(functools.partial(relay_kernel, sections, peers), out_shap...  102 us
    pallas_call x1, Pallas kernels, handed_over(): pl.pallas_call(copy_kernel, out_shape=(jax.ShapeDtypeStruct(first.shape,...  80.5 us
    pallas_call x1, Pallas kernels, pick(): pl.pallas_call(pick_kernel, out_shape=jax.ShapeDtypeStruct((plan.shape[1]...  5.75 us

profile of v2, /device:TPU:8, one launch (start us, length us, event | category | flops | bytes accessed | tf_op | source)
XLA Modules:
  0.0 190.2 jit_solution(9496478990304808880)
XLA Ops:
  1.3 5.8 %shard_map.68.picked = bf16[128,512]{1,0:T(8,128)(2,1)} custom-call(s32[1,2]{1,0:T(1,128)} %plan.1, s32[1]{0:T(128)S(6)} %copy.7.block, bf16[1,3,64,8192]{3,2,1,0:T(8,128)(2,1)} %saved.1), custom_call_target="tpu_custom_call" | custom-call | tf_op jit(solution)/shard_map/pallas_call | solution.py:361
  7.0 102.4 %shard_map.69 = (bf16[1,2,64,8192]{3,2,1,0:T(8,128)(2,1)}, bf16[1,512,512]{2,1,0:T(8,128)(2,1)}) custom-call(bf16[1,2,64,8192]{3,2,1,0:T(8,128)(2,1)} %grads.1, bf16[1,2048,8192]{2,1,0:T(8,128)(2,1)} %weights.1, bf16[128,512]{1,0:T(8,128)(2,1)} %shard_map.68.picked), custom_call_target="tpu_custom_call" | custom-call | flops 17179869184 | bytes 33554432 | tf_op jit(solution)/shard_map/pallas_call | solution.py:280
  109.5 80.5 %shard_map.70 = (bf16[1,2,64,8192]{3,2,1,0:T(8,128)(2,1)}, bf16[1,512,512]{2,1,0:T(8,128)(2,1)}) custom-call(bf16[1,2,64,8192]{3,2,1,0:T(8,128)(2,1)} %get-tuple-element.4.first, bf16[1,512,512]{2,1,0:T(8,128)(2,1)} %get-tuple-element.5.second), custom_call_target="tpu_custom_call" | custom-call | tf_op jit(solution)/shard_map/pallas_call | solution.py:330
